TPU v7x, 256 devices: a whole 4x4x8 slice. The times are simulated.
256 devices in a mesh: dp: 16 (over z, core), mp: 16 (over x, y).
Axes of the slice: x: 4, y: 4, z: 8, core: 2. Of those that a mesh axis runs over, the one named last changes fastest.
Arguments:
- tokens: bfloat16 [12288, 2304], P('dp'), may hold values from -6 to 6
- up_cotangent: bfloat16 [12288, 18432], P('dp', 'mp'), may hold values from -0.59765625 to 0.59765625
- up_weight: bfloat16 [2304, 18432], P('dp', 'mp'), may hold values from -0.1875 to 0.1875
- carried: bfloat16 [16, 2304, 18432], P('dp', None, 'mp'), may hold values from -12 to 12
- momentum: float32 [2304, 18432], P('dp', 'mp'), may hold values from -3 to 3
- q_start: float32 [18432, 64], P('mp'), may hold values from -6 to 6
Outputs:
- feature_grad: float32 [12288, 2304], P('dp', 'mp')
- right_factor: float32 [18432, 64], P('mp')
- new_momentum: float32 [2304, 18432], P('dp', 'mp')
All inputs are finite; a program needn't handle non-finite values.
Results may differ from a plain program's by a relative error of at most 0.0003.
Values may be sent and summed in bfloat16 or wider, within the bound.
A program may use at most 128 MiB of HBM per device.

v0:
```python
import jax
import jax.numpy as jnp
from jax import lax
from jax.sharding import PartitionSpec as P

decay_rate = 0.9


def triangle_apply(rows, gram):
    lower = jnp.linalg.cholesky(gram)
    return jax.scipy.linalg.solve_triangular(lower, rows.T, lower=True).T


def gram_of(rows):
    return jnp.dot(rows.T, rows, precision=lax.Precision.HIGHEST)


def body(tokens, up_cotangent, up_weight, carried, momentum, q_start):
    share = 1.0 / lax.axis_size("dp")
    slab_rows = momentum.shape[0]
    partial_value = lax.dot_general(
        up_cotangent,
        lax.all_gather(up_weight, "dp", axis=0, tiled=True),
        (((1,), (1,)), ((), ())),
        preferred_element_type=jnp.float32,
    )
    feature_grad = lax.psum_scatter(partial_value, "mp", scatter_dimension=1, tiled=True)
    error_rows = carried[0]
    grads = lax.dot_general(
        tokens, up_cotangent, (((0,), (0,)), ((), ())), preferred_element_type=jnp.float32
    )
    whole = error_rows.astype(jnp.float32) + grads
    left_part = jnp.dot(whole, q_start, precision=lax.Precision.HIGHEST) * share
    left = lax.psum(left_part, "dp")
    basis = triangle_apply(left, gram_of(left))
    own_rows = lax.dynamic_slice_in_dim(basis, lax.axis_index("dp") * slab_rows, slab_rows, 0)
    right_part = lax.dot_general(
        whole, basis, (((0,), (0,)), ((), ())), precision=lax.Precision.HIGHEST
    )
    right_factor = lax.psum(right_part * share, "dp")
    decoded = jnp.dot(own_rows, right_factor.T, precision=lax.Precision.HIGHEST)
    new_momentum = decay_rate * momentum + decoded
    return (feature_grad, right_factor, new_momentum)


def solution(mesh):
    placed = (
        P("dp", None),
        P("dp", "mp"),
        P("dp", "mp"),
        P("dp", None, "mp"),
        P("dp", "mp"),
        P("mp", None),
    )
    return jax.shard_map(
        body,
        mesh=mesh,
        in_specs=placed,
        out_specs=(P("dp", "mp"), P("mp", None), P("dp", "mp")),
        check_vma=False,
    )
```

profile of v0, /device:TPU:12, one launch (start us, length us, event | category | flops | bytes accessed | tf_op | source)
XLA Modules:
  0.0 394.8 jit_solution(10951884973813700216)
XLA Ops:
  7.2 0.0 copy-start
  7.2 0.0 all-reduce.3.cloned.1.call-start
  7.2 1.9 copy-done
  9.2 7.6 %convolution_add_fusion = f32[2304,1152]{1,0:T(8,128)S(1)} fusion(bf16[768,2304]{1,0:T(8,128)(2,1)S(1)} %copy-done, bf16[768,1152]{1,0:T(8,128)(2,1)} %param.7, bf16[1,2304,1152]{2,1,0:T(8,128)(2,1)} %param.9), kind=kOutput, calls=%fused_computation | convolution fusion | flops 4082171904 | bytes 21233664 | tf_op jit(solution)/shard_map/dot_general | solution.py:29
  16.8 0.0 copy-start.1
  16.8 4.0 %copy-done.1 = f32[2304,1152]{1,0:T(8,128)} copy-done((f32[2304,1152]{1,0:T(8,128)}, f32[2304,1152]{1,0:T(8,128)S(1)}, u32[]{:S(2)}) %copy-start.1) | copy-done | bytes 10616856
  20.8 11.3 %convolution_multiply_fusion = f32[2304,64]{0,1:T(8,128)} fusion(f32[2304,1152]{1,0:T(8,128)S(1)} %convolution_add_fusion, f32[1152,64]{0,1:T(8,128)S(1)} %copy-done.3), kind=kOutput, calls=%fused_computation.1 | convolution fusion | flops 2038579200 | bytes 11501568 | tf_op jit(solution)/shard_map/dot_general | solution.py:33
  32.1 0.0 all-reduce.3.cloned.1.call-update
  32.1 0.0 all-gather.2.cloned.1.call-start
  32.2 0.7 all-gather.2.cloned.1.call-update
  32.9 0.2 all-reduce.5.cloned.1.call-start
  33.1 111.8 %all-reduce.3.cloned.1.call-done = f32[2304,64]{0,1:T(8,128)} async-done(((f32[2304,64]{0,1:T(8,128)}), f32[2304,64]{0,1:T(8,128)}) %all-reduce.3.cloned.1.call-update) | async-done | bytes 589840 | tf_op jit(solution)/shard_map/psum | solution.py:34
  144.9 2.5 fusion.7
  147.4 1.5 copy.9
  148.9 1.4 fusion.4
  150.3 7.2 %cholesky.16 = f32[64,64]{1,0:T(8,128)} custom-call(f32[64,64]{1,0:T(8,128)} %fusion.4), custom_call_target="Cholesky" | custom-call | tf_op jit(solution)/shard_map/jit(cholesky)/cholesky | solution.py:10
  157.5 0.8 select_reduce_fusion
  158.3 0.6 compare_reduce_fusion
  158.9 2.0 fusion.1
  160.9 6.3 %custom-call.7 = f32[1,64,64]{1,2,0:T(8,128)} custom-call(f32[1,64,64]{2,1,0:T(8,128)} %fusion.1), custom_call_target="InvertDiagBlocksLowerTriangular" | custom-call | tf_op jit(solution)/shard_map/jit(_solve_triangular)/triangular_solve | solution.py:11
  167.2 1.8 fusion.2
  169.0 0.8 copy-done.2
  169.9 9.3 %convolution_multiply_fusion.1 = f32[1152,64]{0,1:T(8,128)} fusion(f32[2304,1152]{1,0:T(8,128)} %copy-done.1, f32[64,2304]{1,0:T(8,128)S(1)} %fusion.2), kind=kOutput, calls=%fused_computation.3 | convolution fusion | flops 2038505472 | bytes 11501568 | tf_op jit(solution)/shard_map/dot_general | solution.py:37
  179.2 0.0 all-reduce.5.cloned.1.call-update
  179.2 0.0 reduce-scatter.2.cloned.1.call-start
  179.3 10.4 %all-gather.2.cloned.1.call-done = bf16[2304,1152]{1,0:T(8,128)(2,1)} async-done(((bf16[144,1152]{1,0:T(8,128)(2,1)}), bf16[2304,1152]{1,0:T(8,128)(2,1)}) %all-gather.2.cloned.1.call-update) | async-done | bytes 5308432 | tf_op jit(solution)/shard_map/all_gather | solution.py:23
  189.6 10.8 %fusion.6 = f32[768,2304]{0,1:T(8,128)} fusion(bf16[768,1152]{1,0:T(8,128)(2,1)} %param.7, bf16[2304,1152]{1,0:T(8,128)(2,1)} %all-gather.2.cloned.1.call-done), kind=kOutput, calls=%fused_computation.16 | convolution fusion | flops 4076863488 | bytes 14155776 | tf_op jit(solution)/shard_map/dot_general | solution.py:21
  200.4 0.0 reduce-scatter.2.cloned.1.call-update
  200.4 95.7 %all-reduce.5.cloned.1.call-done = f32[1152,64]{0,1:T(8,128)} async-done(((f32[1152,64]{0,1:T(8,128)}), f32[1152,64]{0,1:T(8,128)}) %all-reduce.5.cloned.1.call-update) | async-done | bytes 294928 | tf_op jit(solution)/shard_map/psum | solution.py:40
  296.2 2.9 convolution_add_fusion.1
  299.0 87.6 %reduce-scatter.2.cloned.1.call-done = f32[768,144]{0,1:T(8,128)} async-done(((f32[768,2304]{0,1:T(8,128)}), f32[768,144]{0,1:T(8,128)}) %reduce-scatter.2.cloned.1.call-update) | async-done | bytes 442384 | tf_op jit(solution)/shard_map/reduce_scatter | solution.py:27
  386.6 1.7 copy.12
  (3 shorter events, 0.0 us)
Async XLA Ops:
  7.2 2.0 copy-start
  7.2 137.8 %all-reduce.3.cloned.1.call-start = ((), (), s32[]{:S(2)}) async-start(), calls=%async_computation.3 | async-start | bytes 1179648 | tf_op jit(solution)/shard_map/psum | solution.py:34
  9.2 11.7 %copy-start.3 = (f32[1152,64]{0,1:T(8,128)S(1)}, f32[1152,64]{0,1:T(8,128)}, u32[]{:S(2)}) copy-start(f32[1152,64]{0,1:T(8,128)} %param.11) | copy-start | bytes 884740
  16.8 4.0 %copy-start.1 = (f32[2304,1152]{1,0:T(8,128)}, f32[2304,1152]{1,0:T(8,128)S(1)}, u32[]{:S(2)}) copy-start(f32[2304,1152]{1,0:T(8,128)S(1)} %convolution_add_fusion) | copy-start | bytes 31850500
  32.1 157.5 %all-gather.2.cloned.1.call-start = ((), (), s32[]{:S(2)}) async-start(), calls=%async_computation.1 | async-start | bytes 5640192 | tf_op jit(solution)/shard_map/all_gather | solution.py:23
  32.9 263.3 %all-reduce.5.cloned.1.call-start = ((), (), s32[]{:S(2)}) async-start(), calls=%async_computation.4 | async-start | bytes 589824 | tf_op jit(solution)/shard_map/psum | solution.py:40
  169.0 0.9 copy-start.2
  179.2 207.4 %reduce-scatter.2.cloned.1.call-start = ((), (), s32[]{:S(2)}) async-start(), calls=%async_computation.2 | async-start | bytes 7520256 | tf_op jit(solution)/shard_map/reduce_scatter | solution.py:27
Sparse Core Ops, SparseCore 0:
  32.3 112.6 all-reduce.2
  146.9 42.6 all-gather.1
  192.6 103.4 all-reduce.4
  300.3 86.2 reduce-scatter.1
where the time goes:
time: 397 us; the launch traced here: 395 us
  waiting for transfers between devices  306 us (77%)
  matrix products  46.1 us (12%)
  other arithmetic  18.4 us (5%)
  between operations  13.8 us (3%)
  local copies, waits for them, and re-layouts  9.96 us (3%)
    psum x1, waiting for transfers between devices, body(): left = lax.psum(left_part, 'dp')  112 us
    psum x1, waiting for transfers between devices, body(): right_factor = lax.psum(right_part * share, 'dp')  95.7 us
    reduce_scatter x1, waiting for transfers between devices, body(): lax.psum_scatter(partial_value, 'mp', scatter_dimension=1, tiled=True)  87.6 us
    dot_general x1, matrix products, body(): left_part = jnp.dot(whole, q_start, precision=lax.Precision.HIGHEST) * share  11.3 us
    dot_general x1, matrix products, body(): lax.dot_general(up_cotangent, lax.all_gather(up_weight, 'dp', axis=0, til...  10.8 us
    all_gather x1, waiting for transfers between devices, body(): lax.all_gather(up_weight, 'dp', axis=0, tiled=True)  10.4 us
    dot_general x1, matrix products, body(): lax.dot_general(whole, basis, (((0,), (0,)), ((), ())), precision=lax.Pre...  9.33 us
    another operation x3, other arithmetic, triangle_apply(): lower = jnp.linalg.cholesky(gram)  8.65 us
  transfers between devices with their start and end apart: 4, of which 4 were waited for; matrix products, arithmetic and copies ran while one was open for 12% of the time, Pallas kernels for 0%

commit v1 on v0

v1 whole, which is shorter than its diff:
```python
import jax
import jax.numpy as jnp
from jax import lax
from jax.experimental import pallas as pl
from jax.experimental.pallas import tpu as pltpu
from jax.sharding import PartitionSpec as P

DECAY = 0.9
MESH = pl.DeviceIdType.MESH
NT = (((1,), (1,)), ((), ()))
NN = (((1,), (0,)), ((), ()))
TN = (((0,), (0,)), ((), ()))
NZ = 8
NDP = 16
RANK = 64
TILE = 384
FAR_FIRST = (4, 3, 5, 2, 6, 1, 7)


def mm(a, b, dims):
    return lax.dot_general(a, b, dims, preferred_element_type=jnp.float32)


def mm32(a, b, dims):
    return lax.dot_general(
        a, b, dims, precision=lax.Precision.HIGHEST, preferred_element_type=jnp.float32
    )


def split3(x):
    hi = x.astype(jnp.bfloat16)
    rest = x - hi.astype(jnp.float32)
    mid = rest.astype(jnp.bfloat16)
    low = (rest - mid.astype(jnp.float32)).astype(jnp.bfloat16)
    return jnp.concatenate([hi, mid, low], axis=0)


def fold3(x):
    return x[0:RANK] + x[RANK : 2 * RANK] + x[2 * RANK :]


def aligned(i, n):
    return pl.multiple_of(i * n, n)


def compress_kernel(
    tokens_hbm, cot_hbm, carried_hbm, momentum_hbm, q_ref,
    right_ref, mom_ref,
    tokens, cot, carried, momentum, q3, t3, lp, sib_l, cs, rsl, left, left3,
    yp, sib_y, ys, rsy, yf, elim,
    load_sem, sib_sem, rs_s, rs_r, ag_s, ag_r, yrs_s, yrs_r, yag_s, yag_r,
):
    dp = lax.axis_index("dp")
    mp = lax.axis_index("mp")
    z, c = dp // 2, dp % 2
    sib = (z * 2 + 1 - c, mp)

    def zdev(d):
        return ((z + d) % NZ * 2 + c, mp)

    loads = [
        pltpu.make_async_copy(src, dst, load_sem.at[i])
        for i, (src, dst) in enumerate(
            ((cot_hbm, cot), (tokens_hbm, tokens), (carried_hbm, carried), (momentum_hbm, momentum))
        )
    ]
    for copy in loads:
        copy.start()
    barrier = pltpu.get_barrier_semaphore()
    pl.semaphore_signal(barrier, inc=1, device_id=sib, device_id_type=MESH)
    for d in range(1, NZ):
        pl.semaphore_signal(barrier, inc=1, device_id=zdev(d), device_id_type=MESH)

    q3[...] = split3(q_ref[...])
    loads[0].wait()
    for t in range(2):
        rows = pl.ds(t * TILE, TILE)
        t3[:, rows] = split3(fold3(mm(q3[...], cot[rows, :], NT)))
    loads[1].wait()
    loads[2].wait()

    def left_tile(t, _):
        columns = pl.ds(aligned(t, TILE), TILE)
        part = mm(q3[...], carried[columns, :], NT) + mm(t3[...], tokens[:, columns], NN)
        lp[t // 3, :, pl.ds(aligned(t % 3, TILE), TILE)] = fold3(part)
        return 0

    lax.fori_loop(0, 6, left_tile, 0)
    pl.semaphore_wait(barrier, NZ)

    def exchange(src, dst, slot):
        return pltpu.make_async_remote_copy(
            src_ref=src, dst_ref=dst, send_sem=sib_sem.at[2 * slot], recv_sem=sib_sem.at[2 * slot + 1],
            device_id=sib, device_id_type=MESH,
        )

    def scatter(src, dst, send, recv):
        copies = []
        for d in FAR_FIRST:
            copy = pltpu.make_async_remote_copy(
                src_ref=src.at[pl.ds(aligned((z + d) % NZ, 8), 8), :], dst_ref=dst.at[d],
                send_sem=send.at[d], recv_sem=recv.at[d], device_id=zdev(d), device_id_type=MESH,
            )
            copy.start()
            copies.append(copy)
        return copies

    def gather(block_of, send, recv):
        copies, arrivals = [], []
        for d in FAR_FIRST:
            copy = pltpu.make_async_remote_copy(
                src_ref=block_of(z), dst_ref=block_of(z),
                send_sem=send.at[d], recv_sem=recv.at[d], device_id=zdev(d), device_id_type=MESH,
            )
            copy.start()
            copies.append(copy)
            arrivals.append(
                pltpu.make_async_remote_copy(
                    src_ref=block_of(z), dst_ref=block_of((z - d + NZ) % NZ),
                    send_sem=send.at[d], recv_sem=recv.at[d], device_id=zdev(d), device_id_type=MESH,
                )
            )
        return copies, arrivals

    pair = exchange(lp.at[1 - c], sib_l, 0)
    pair.start()
    pair.wait()
    cs[...] = lp[c] + sib_l[...]
    copies = scatter(cs, rsl, rs_s, rs_r)
    own_rows = pl.ds(aligned(z, 8), 8)
    total = cs[own_rows, :]
    for copy in copies:
        copy.wait_recv()
    for d in range(1, NZ):
        total = total + rsl[d]
    left[c, own_rows, :] = total * (1.0 / NDP)
    for copy in copies:
        copy.wait_send()
    copies, arrivals = gather(lambda j: left.at[c, pl.ds(aligned(j, 8), 8), :], ag_s, ag_r)
    for copy in arrivals:
        copy.wait_recv()
    for copy in copies:
        copy.wait_send()
    pair = exchange(left.at[c], left.at[c], 1)
    pair.start()
    back = exchange(left.at[c], left.at[1 - c], 1)
    back.wait_recv()
    pair.wait_send()

    for h in range(2):
        left3[:, h * 1152 : (h + 1) * 1152] = split3(left[h])
    for t in range(2):
        rows = pl.ds(t * TILE, TILE)
        t3[:, rows] = split3(fold3(mm(left3[...], tokens[rows, :], NT)))

    def y_tile(t, _):
        columns = pl.ds(aligned(t, TILE), TILE)
        part = mm(left3[...], carried[:, columns], NN) + mm(t3[...], cot[:, columns], NN)
        yp[:, columns] = fold3(part)
        return 0

    lax.fori_loop(0, 3, y_tile, 0)

    def mine(core):
        return pl.ds(pl.multiple_of(core * 512, 128), 640)

    pair = exchange(yp.at[:, mine(1 - c)], sib_y, 2)
    pair.start()
    pair.wait()
    ys[...] = yp[:, mine(c)] + sib_y[...]
    copies = scatter(ys, rsy, yrs_s, yrs_r)

    products = mm(left3[...], left3[...], NT)
    gram = jnp.zeros((RANK, RANK), jnp.float32)
    for i in (2, 1, 0):
        for j in (2, 1, 0):
            gram = gram + products[i * RANK : (i + 1) * RANK, j * RANK : (j + 1) * RANK]
    row_id = lax.broadcasted_iota(jnp.int32, (RANK, 2 * RANK), 0)
    lane_id = lax.broadcasted_iota(jnp.int32, (RANK, 2 * RANK), 1)
    elim[:, 0:RANK] = gram
    elim[:, RANK:] = jnp.where(row_id[:, 0:RANK] == lane_id[:, 0:RANK], 1.0, 0.0)

    def eliminate(j, _):
        row = elim[pl.ds(j, 1), :]
        full = elim[...]
        pivot = jnp.sum(jnp.where(lane_id[0:1] == j, row, 0.0), axis=1, keepdims=True)
        column = jnp.sum(jnp.where(lane_id == j, full, 0.0), axis=1, keepdims=True)
        factor = jnp.where(row_id[:, 0:1] > j, column / pivot, 0.0)
        elim[...] = full - factor * row
        return 0

    lax.fori_loop(0, RANK - 1, eliminate, 0)
    done = elim[...]
    diagonal = jnp.sum(jnp.where(lane_id == row_id, done, 0.0), axis=1, keepdims=True)
    inverse = done[:, RANK:] / jnp.sqrt(diagonal)
    k = dp % 8
    window = left[dp // 8, :, pl.ds(aligned(k, 128), 256)]
    own_left = pltpu.roll(window, (256 - 16 * k) % 256, 1)[:, 0:144]
    own_basis = mm32(inverse, own_left, NN)

    total = ys[own_rows, :]
    for copy in copies:
        copy.wait_recv()
    for d in range(1, NZ):
        total = total + rsy[d]
    yf[own_rows, mine(c)] = total
    for copy in copies:
        copy.wait_send()
    copies, arrivals = gather(lambda j: yf.at[pl.ds(aligned(j, 8), 8), mine(c)], yag_s, yag_r)
    for copy in arrivals:
        copy.wait_recv()
    for copy in copies:
        copy.wait_send()

    def given(core):
        return yf.at[:, pl.ds(pl.multiple_of(core * 640, 128), 512)]

    pair = exchange(given(c), given(c), 3)
    pair.start()
    back = exchange(given(c), given(1 - c), 3)
    back.wait_recv()
    pair.wait_send()
    loads[3].wait()
    for t in range(3):
        columns = pl.ds(t * TILE, TILE)
        right = mm32(inverse, yf[:, columns], NN) * (1.0 / NDP)
        right_ref[:, columns] = right
        mom_ref[:, columns] = DECAY * momentum[:, columns] + mm32(own_basis, right, TN)


def compress(tokens, cot, carried, momentum, q_t):
    f32, bf16 = jnp.float32, jnp.bfloat16
    dma = pltpu.SemaphoreType.DMA
    hbm = pl.BlockSpec(memory_space=pl.ANY)
    vmem = pl.BlockSpec(memory_space=pltpu.VMEM)
    return pl.pallas_call(
        compress_kernel,
        out_shape=(
            jax.ShapeDtypeStruct((RANK, 1152), f32),
            jax.ShapeDtypeStruct((144, 1152), f32),
        ),
        in_specs=[hbm] * 4 + [vmem],
        out_specs=(vmem, vmem),
        scratch_shapes=[
            pltpu.VMEM((768, 2304), bf16),
            pltpu.VMEM((768, 1152), bf16),
            pltpu.VMEM((2304, 1152), bf16),
            pltpu.VMEM((144, 1152), f32),
            pltpu.VMEM((192, 1152), bf16),
            pltpu.VMEM((192, 768), bf16),
            pltpu.VMEM((2, RANK, 1152), f32),
            pltpu.VMEM((RANK, 1152), f32),
            pltpu.VMEM((RANK, 1152), f32),
            pltpu.VMEM((NZ, 8, 1152), f32),
            pltpu.VMEM((2, RANK, 1152), f32),
            pltpu.VMEM((192, 2304), bf16),
            pltpu.VMEM((RANK, 1152), f32),
            pltpu.VMEM((RANK, 640), f32),
            pltpu.VMEM((RANK, 640), f32),
            pltpu.VMEM((NZ, 8, 640), f32),
            pltpu.VMEM((RANK, 1152), f32),
            pltpu.VMEM((RANK, 128), f32),
            dma((4,)),
            dma((8,)),
        ]
        + [dma((NZ,))] * 8,
        compiler_params=pltpu.CompilerParams(
            collective_id=0, has_side_effects=True, vmem_limit_bytes=48 * 2**20
        ),
        cost_estimate=pl.CostEstimate(
            flops=4 * 10**9, bytes_accessed=12 * 10**6, transcendentals=0
        ),
        name="compress",
    )(tokens, cot, carried, momentum, q_t)


def body(tokens, up_cotangent, up_weight, carried, momentum, q_start):
    partial_value = lax.dot_general(
        up_cotangent,
        lax.all_gather(up_weight, "dp", axis=0, tiled=True),
        (((1,), (1,)), ((), ())),
        preferred_element_type=jnp.float32,
    )
    feature_grad = lax.psum_scatter(partial_value, "mp", scatter_dimension=1, tiled=True)
    right_t, new_momentum = compress(tokens, up_cotangent, carried[0], momentum, q_start.T)
    return (feature_grad, right_t.T, new_momentum)


def solution(mesh):
    placed = (
        P("dp", None),
        P("dp", "mp"),
        P("dp", "mp"),
        P("dp", None, "mp"),
        P("dp", "mp"),
        P("mp", None),
    )
    return jax.shard_map(
        body,
        mesh=mesh,
        in_specs=placed,
        out_specs=(P("dp", "mp"), P("mp", None), P("dp", "mp")),
        check_vma=False,
    )
```

time: 397 us -> 162 us (0.41)
  waiting for transfers between devices: 306 us -> 81.3 us
  Pallas kernels: 0 us -> 49.9 us
  matrix products: 46.1 us -> 10.8 us
  other arithmetic: 18.4 us -> 0 us
  local copies, waits for them, and re-layouts: 9.96 us -> 4.11 us
    psum x2 -> x0, waiting for transfers between devices: 208 us -> none  [the longest x1 112 us: body(): left = lax.psum(left_part, 'dp')]
    reduce_scatter x1, waiting for transfers between devices: 87.6 us -> 32.4 us  [body(): lax.psum_scatter(partial_value, 'mp', scatter_dimension=1, tiled=True)]
    pallas_call x0 -> x1, Pallas kernels: none -> 49.9 us  [compress(): pl.pallas_call(compress_kernel, out_shape=(jax.ShapeDtypeStruct((RANK, 11...]
    all_gather x1, waiting for transfers between devices: 10.4 us -> 48.2 us  [body(): lax.all_gather(up_weight, 'dp', axis=0, tiled=True)]
    dot_general x5 -> x0, matrix products: 33.6 us -> none  [the longest x1 11.3 us: body(): left_part = jnp.dot(whole, q_start, precision=lax.Precision.HIGHEST) * share]
    another operation x5 -> x0, other arithmetic: 17 us -> none  [the longest x3 8.65 us: triangle_apply(): lower = jnp.linalg.cholesky(gram)]
    unnamed x9 -> x8, local copies, waits for them, and re-layouts: 8.5 us -> 4.11 us
  transfers between devices with their start and end apart: 4 -> 2, of which waited for: 4 -> 2; matrix products, arithmetic and copies ran while one was open for 12% -> 0% of each run, Pallas kernels for 0% -> 31%
where the time goes in v1:
time: 162 us; the launch traced here: 160 us
  waiting for transfers between devices  81.3 us (50%)
  Pallas kernels  49.9 us (31%)
  between operations  14 us (9%)
  matrix products  10.8 us (7%)
  local copies, waits for them, and re-layouts  4.11 us (3%)
    pallas_call x1, Pallas kernels, compress(): pl.pallas_call(compress_kernel, out_shape=(jax.ShapeDtypeStruct((RANK, 11...  49.9 us
    all_gather x1, waiting for transfers between devices, body(): lax.all_gather(up_weight, 'dp', axis=0, tiled=True)  48.2 us
    reduce_scatter x1, waiting for transfers between devices, body(): lax.psum_scatter(partial_value, 'mp', scatter_dimension=1, tiled=True)  32.4 us
    dot_general x1, matrix products, body(): lax.dot_general(up_cotangent, lax.all_gather(up_weight, 'dp', axis=0, til...  10.8 us
    unnamed x8, local copies, waits for them, and re-layouts  4.11 us
  transfers between devices with their start and end apart: 2, of which 2 were waited for; matrix products, arithmetic and copies ran while one was open for 0% of the time, Pallas kernels for 31%

profile of v1, /device:TPU:12, one launch (start us, length us, event | category | flops | bytes accessed | tf_op | source)
XLA Modules:
  0.0 160.2 jit_solution(11500644735227331)
XLA Ops:
  7.2 0.0 all-gather.2.cloned.1.call-start
  7.2 0.7 all-gather.2.cloned.1.call-update
  7.9 0.0 reduce-scatter.2.cloned.1.call-start
  7.9 48.2 %all-gather.2.cloned.1.call-done = bf16[2304,1152]{1,0:T(8,128)(2,1)} async-done(((bf16[144,1152]{1,0:T(8,128)(2,1)}), bf16[2304,1152]{1,0:T(8,128)(2,1)}) %all-gather.2.cloned.1.call-update) | async-done | bytes 5308432 | tf_op jit(solution)/shard_map/all_gather | solution.py:280
  56.1 10.8 %fusion = f32[768,2304]{0,1:T(8,128)} fusion(bf16[768,1152]{1,0:T(8,128)(2,1)} %cot_hbm.1, bf16[2304,1152]{1,0:T(8,128)(2,1)} %all-gather.2.cloned.1.call-done), kind=kOutput, calls=%fused_computation | convolution fusion | flops 4076863488 | bytes 14155776 | tf_op jit(solution)/shard_map/dot_general | solution.py:278
  66.9 0.0 copy-start
  66.9 0.0 copy-start.1
  66.9 0.0 reduce-scatter.2.cloned.1.call-update
  66.9 1.4 copy-done
  68.4 0.1 copy-done.1
  68.5 0.0 copy-start.2
  68.5 1.0 copy-done.2
  69.5 49.9 %compress.1 = (f32[64,1152]{1,0:T(8,128)S(1)}, f32[144,1152]{1,0:T(8,128)S(1)}) custom-call(bf16[768,2304]{1,0:T(8,128)(2,1)} %tokens_hbm.1, bf16[768,1152]{1,0:T(8,128)(2,1)S(1)} %copy-done, bf16[2304,1152]{1,0:T(8,128)(2,1)} %bitcast.7, f32[144,1152]{1,0:T(8,128)S(1)} %copy-done.1, f32[64,1152]{1,0:T(8,128)S(1)} %bitcast.6), custom_call_target="tpu_custom_call" | custom-call | flops 4000000000 | bytes 12000000 | tf_op jit(solution)/shard_map/compress/pallas_call | solution.py:236
  119.4 32.4 %reduce-scatter.2.cloned.1.call-done = f32[768,144]{0,1:T(8,128)} async-done(((f32[768,2304]{0,1:T(8,128)}), f32[768,144]{0,1:T(8,128)}) %reduce-scatter.2.cloned.1.call-update) | async-done | bytes 442384 | tf_op jit(solution)/shard_map/reduce_scatter | solution.py:284
  151.8 0.7 copy.11
  152.5 0.8 copy.12
Async XLA Ops:
  7.2 49.0 %all-gather.2.cloned.1.call-start = ((), (), s32[]{:S(2)}) async-start(), calls=%async_computation.1 | async-start | bytes 5640192 | tf_op jit(solution)/shard_map/all_gather | solution.py:280
  7.9 143.9 %reduce-scatter.2.cloned.1.call-start = ((), (), s32[]{:S(2)}) async-start(), calls=%async_computation.2 | async-start | bytes 7520256 | tf_op jit(solution)/shard_map/reduce_scatter | solution.py:284
  66.9 1.5 copy-start
  66.9 1.6 %copy-start.1 = (f32[144,1152]{1,0:T(8,128)S(1)}, f32[144,1152]{1,0:T(8,128)}, u32[]{:S(2)}) copy-start(f32[144,1152]{1,0:T(8,128)} %momentum_hbm.1) | copy-start | bytes 1990660
  68.5 1.0 copy-start.2
Sparse Core Ops, SparseCore 0:
  9.8 46.2 all-gather.1
  67.0 84.7 reduce-scatter.1

commit v2 on v1

v2 whole, which is shorter than its diff:
```python
import jax
import jax.numpy as jnp
from jax import lax
from jax.experimental import pallas as pl
from jax.experimental.pallas import tpu as pltpu
from jax.sharding import PartitionSpec as P

DECAY = 0.9
MESH = pl.DeviceIdType.MESH
NT = (((1,), (1,)), ((), ()))
NN = (((1,), (0,)), ((), ()))
TN = (((0,), (0,)), ((), ()))
NZ = 8
NDP = 16
RANK = 64
TILE = 384
FAR_FIRST = (4, 3, 5, 2, 6, 1, 7)
CHUNK = 144
HALF = 72
SPLIT = 80


def mm(a, b, dims):
    return lax.dot_general(a, b, dims, preferred_element_type=jnp.float32)


def mm32(a, b, dims):
    return lax.dot_general(
        a, b, dims, precision=lax.Precision.HIGHEST, preferred_element_type=jnp.float32
    )


def split3(x):
    hi = x.astype(jnp.bfloat16)
    rest = x - hi.astype(jnp.float32)
    mid = rest.astype(jnp.bfloat16)
    low = (rest - mid.astype(jnp.float32)).astype(jnp.bfloat16)
    return jnp.concatenate([hi, mid, low], axis=0)


def fold3(x):
    return x[0:RANK] + x[RANK : 2 * RANK] + x[2 * RANK :]


def aligned(i, n):
    return pl.multiple_of(i * n, n)


def fused_kernel(
    tokens_hbm, cot_hbm, weight_hbm, carried_hbm, momentum_hbm, q_ref,
    feature_ref, right_ref, mom_ref,
    tokens, cot, carried, momentum, q3, t3, lp, sib_l, cs, rsl, left, left3,
    yp, sib_y, ys, rsy, yf, elim,
    weight, part, r1, rl1, r2, rl2,
    load_sem, sib_sem, rs_s, rs_r, ag_s, ag_r, yrs_s, yrs_r, yag_s, yag_r,
    w_s, w_r, ws_s, ws_r, f1_s, r1_r, rl1_r, f2_s, r2_r, rl2_r,
):
    dp = lax.axis_index("dp")
    mp = lax.axis_index("mp")
    z, c = dp // 2, dp % 2
    x, y = mp // 4, mp % 4
    sib = (z * 2 + 1 - c, mp)

    def zdev(d):
        return ((z + d) % NZ * 2 + c, mp)

    def xydev(axis, d):
        if axis == 0:
            return (dp, (x + d) % 4 * 4 + y)
        return (dp, x * 4 + (y + d) % 4)

    def remote(src, dst, send, recv, device):
        return pltpu.make_async_remote_copy(
            src_ref=src, dst_ref=dst, send_sem=send, recv_sem=recv,
            device_id=device, device_id_type=MESH,
        )

    own_chunk = pl.ds(pl.multiple_of(dp * CHUNK, 16), CHUNK)
    loads = [
        pltpu.make_async_copy(src, dst, load_sem.at[i])
        for i, (src, dst) in enumerate(
            (
                (weight_hbm, weight.at[own_chunk, :]), (cot_hbm, cot), (tokens_hbm, tokens),
                (carried_hbm, carried), (momentum_hbm, momentum),
            )
        )
    ]
    for copy in loads:
        copy.start()
    barrier = pltpu.get_barrier_semaphore()
    pl.semaphore_signal(barrier, inc=1, device_id=sib, device_id_type=MESH)
    for d in FAR_FIRST:
        pl.semaphore_signal(barrier, inc=1, device_id=zdev(d), device_id_type=MESH)
    for axis in range(2):
        for d in (1, 3):
            pl.semaphore_signal(barrier, inc=1, device_id=xydev(axis, d), device_id_type=MESH)

    def weight_rows(way, s, core, first=0, count=CHUNK):
        place = (z - s + NZ) % NZ if way == 0 else (z + s) % NZ
        return weight.at[pl.ds(pl.multiple_of((place * 2 + core) * CHUNK + first, 16), count), :]

    def ring_copy(way, s):
        first, count = 0, CHUNK
        if s == 4:
            first, count = (0, SPLIT) if way == 0 else (SPLIT, CHUNK - SPLIT)
        src = weight_rows(way, s - 1, c, first, count)
        return remote(src, src, w_s.at[way, s - 1], w_r.at[way, s], zdev(1 if way == 0 else NZ - 1))

    def ring_arrival(way, s):
        first, count = 0, CHUNK
        if s == 4:
            first, count = (0, SPLIT) if way == 0 else (SPLIT, CHUNK - SPLIT)
        dst = weight_rows(way, s, c, first, count)
        return remote(dst, dst, w_s.at[way, s - 1], w_r.at[way, s], zdev(1))

    def pair_copy(way, s, core):
        rows = weight_rows(way, s, core)
        return remote(rows, rows, ws_s.at[way, s], ws_r.at[way, s], sib)

    def ways_of(s):
        return (0,) if s in (0, 4) else (0, 1)

    def ring_step(s):
        for way in (0, 1):
            if s > 0:
                ring_arrival(way, s).wait_recv()
            if s < 4:
                ring_copy(way, s + 1).start()
            if s in (1, 2, 3):
                pair_copy(way, s, c).start()
        if s in (0, 4):
            pair_copy(0, s, c).start()

    def block(h, j, upper):
        return part.at[h, pl.ds(pl.multiple_of(j * CHUNK + (0 if upper else HALF), 8), HALF), :]

    def rows_of(upper):
        return pl.ds(0 if upper else HALF, HALF)

    class Stage:
        def __init__(self, number):
            self.number = number
            self.sends, self.arrive, self.passed = ((f1_s, r1_r, rl1_r), (f2_s, r2_r, rl2_r))[number]
            self.into, self.relay = ((r1, rl1), (r2, rl2))[number]

        def axis(self, h):
            return h if self.number == 0 else 1 - h

        def slot(self, h, j):
            if self.number == 1:
                return 0
            return j % 4 if h == 0 else j // 4

        def distance(self, h, j):
            if self.axis(h) == 0:
                return (j // 4 - x + 4) % 4
            return (j % 4 - y + 4) % 4

        def send(self, h, j, upper, direct, way):
            k = self.slot(h, j)
            source = block(h, j, upper)
            part_id = 0 if upper else 1
            if direct:
                dst = self.into.at[h, way, k, rows_of(upper), :]
                recv = self.arrive.at[h, way, k, part_id]
            else:
                dst = self.relay.at[h, way, k]
                recv = self.passed.at[h, way, k]
            return remote(
                source, dst, self.sends.at[h, j, part_id], recv,
                xydev(self.axis(h), 1 if way == 0 else 3),
            )

        def plain(self, h, j):
            far = self.distance(h, j)

            @pl.when(far == 2)
            def _():
                self.send(h, j, True, False, 0).start()
                self.send(h, j, False, False, 1).start()

            @pl.when(far == 1)
            def _():
                self.send(h, j, False, True, 0).start()

            @pl.when(far == 3)
            def _():
                self.send(h, j, True, True, 1).start()

        def merge(self, h, j):
            far = self.distance(h, j)
            k = self.slot(h, j)

            def one(way, upper):
                rows = block(h, j, upper)
                copy = remote(
                    self.relay.at[h, way, k], self.relay.at[h, way, k],
                    self.sends.at[h, j, 0], self.passed.at[h, way, k], xydev(self.axis(h), 1),
                )
                copy.wait_recv()
                rows[...] = rows[...] + self.relay[h, way, k]
                self.send(h, j, upper, True, way).start()

            @pl.when(far == 1)
            def _():
                one(0, True)

            @pl.when(far == 3)
            def _():
                one(1, False)

        def collect(self, h, j):
            k = self.slot(h, j)
            for way in range(2):
                for upper in (True, False):
                    dst = self.into.at[h, way, k, rows_of(upper), :]
                    remote(
                        dst, dst, self.sends.at[h, j, 0],
                        self.arrive.at[h, way, k, 0 if upper else 1], xydev(self.axis(h), 1),
                    ).wait_recv()
            own = pl.ds(pl.multiple_of(j * CHUNK, 8), CHUNK)
            return part[h, own, :] + self.into[h, 0, k] + self.into[h, 1, k]

        def drain(self, h, j):
            @pl.when(self.distance(h, j) != 0)
            def _():
                for upper in (True, False):
                    self.send(h, j, upper, True, 0).wait_send()

    first, second = Stage(0), Stage(1)

    def place_of(way, s):
        return (z - s + NZ) % NZ if way == 0 else (z + s) % NZ

    def partials(s):
        for way in ways_of(s):
            place = place_of(way, s)
            pair_copy(way, s, 1 - c).wait_recv()
            rows = pl.ds(pl.multiple_of(place * (2 * CHUNK), 16), 2 * CHUNK)
            for h in range(2):
                part[h, rows, :] = mm(weight[rows, :], cot[pl.ds(h * TILE, TILE), :], NT)
            for h in range(2):
                for b in range(2):
                    first.plain(h, place * 2 + b)

    def merges(s):
        for way in ways_of(s):
            for b in range(2):
                for h in range(2):
                    first.merge(h, place_of(way, s) * 2 + b)

    def own_block(h, k):
        return x * 4 + k if h == 0 else k * 4 + y

    def second_start():
        for k in range(4):
            for h in range(2):
                j = own_block(h, k)
                total = first.collect(h, j)
                part[h, pl.ds(pl.multiple_of(j * CHUNK, 8), CHUNK), :] = total
                second.plain(h, j)

    def second_merges():
        for k in range(4):
            for h in range(2):
                second.merge(h, own_block(h, k))

    def feature_finish():
        for h in range(2):
            feature_ref[:, pl.ds(h * TILE, TILE)] = second.collect(h, mp)

    q3[...] = split3(q_ref[...])
    loads[1].wait()
    for t in range(2):
        rows = pl.ds(t * TILE, TILE)
        t3[:, rows] = split3(fold3(mm(q3[...], cot[rows, :], NT)))
    loads[0].wait()
    pl.semaphore_wait(barrier, NZ + 4)
    ring_step(0)

    loads[2].wait()
    loads[3].wait()

    def left_tile(t, _):
        columns = pl.ds(aligned(t, TILE), TILE)
        value = mm(q3[...], carried[columns, :], NT) + mm(t3[...], tokens[:, columns], NN)
        lp[t // 3, :, pl.ds(aligned(t % 3, TILE), TILE)] = fold3(value)
        return 0

    lax.fori_loop(0, 6, left_tile, 0)

    def exchange(src, dst, slot):
        return remote(src, dst, sib_sem.at[2 * slot], sib_sem.at[2 * slot + 1], sib)

    def scatter(src, dst, send, recv):
        copies = []
        for d in FAR_FIRST:
            copy = remote(
                src.at[pl.ds(aligned((z + d) % NZ, 8), 8), :], dst.at[d],
                send.at[d], recv.at[d], zdev(d),
            )
            copy.start()
            copies.append(copy)
        return copies

    def gather(block_of, send, recv):
        copies, arrivals = [], []
        for d in FAR_FIRST:
            copy = remote(block_of(z), block_of(z), send.at[d], recv.at[d], zdev(d))
            copy.start()
            copies.append(copy)
            arrivals.append(
                remote(block_of(z), block_of((z - d + NZ) % NZ), send.at[d], recv.at[d], zdev(d))
            )
        return copies, arrivals

    pair = exchange(lp.at[1 - c], sib_l, 0)
    pair.start()
    partials(0)
    pair.wait()
    cs[...] = lp[c] + sib_l[...]
    copies = scatter(cs, rsl, rs_s, rs_r)
    ring_step(1)
    partials(1)
    merges(0)
    own_rows = pl.ds(aligned(z, 8), 8)
    total = cs[own_rows, :]
    for copy in copies:
        copy.wait_recv()
    for d in range(1, NZ):
        total = total + rsl[d]
    left[c, own_rows, :] = total * (1.0 / NDP)
    for copy in copies:
        copy.wait_send()
    copies, arrivals = gather(lambda j: left.at[c, pl.ds(aligned(j, 8), 8), :], ag_s, ag_r)
    ring_step(2)
    partials(2)
    merges(1)
    for copy in arrivals:
        copy.wait_recv()
    for copy in copies:
        copy.wait_send()
    pair = exchange(left.at[c], left.at[c], 1)
    pair.start()
    ring_step(3)
    exchange(left.at[c], left.at[1 - c], 1).wait_recv()
    pair.wait_send()

    for h in range(2):
        left3[:, h * 1152 : (h + 1) * 1152] = split3(left[h])
    for t in range(2):
        rows = pl.ds(t * TILE, TILE)
        t3[:, rows] = split3(fold3(mm(left3[...], tokens[rows, :], NT)))

    def y_tile(t, _):
        columns = pl.ds(aligned(t, TILE), TILE)
        value = mm(left3[...], carried[:, columns], NN) + mm(t3[...], cot[:, columns], NN)
        yp[:, columns] = fold3(value)
        return 0

    lax.fori_loop(0, 3, y_tile, 0)

    def mine(core):
        return pl.ds(pl.multiple_of(core * 512, 128), 640)

    pair = exchange(yp.at[:, mine(1 - c)], sib_y, 2)
    pair.start()
    partials(3)
    merges(2)
    pair.wait()
    ys[...] = yp[:, mine(c)] + sib_y[...]
    copies = scatter(ys, rsy, yrs_s, yrs_r)
    ring_step(4)
    partials(4)
    merges(3)

    products = mm(left3[...], left3[...], NT)
    gram = jnp.zeros((RANK, RANK), jnp.float32)
    for i in (2, 1, 0):
        for j in (2, 1, 0):
            gram = gram + products[i * RANK : (i + 1) * RANK, j * RANK : (j + 1) * RANK]
    row_id = lax.broadcasted_iota(jnp.int32, (RANK, 2 * RANK), 0)
    lane_id = lax.broadcasted_iota(jnp.int32, (RANK, 2 * RANK), 1)
    elim[:, 0:RANK] = gram
    elim[:, RANK:] = jnp.where(row_id[:, 0:RANK] == lane_id[:, 0:RANK], 1.0, 0.0)

    def eliminate(j, _):
        row = elim[pl.ds(j, 1), :]
        full = elim[...]
        pivot = jnp.sum(jnp.where(lane_id[0:1] == j, row, 0.0), axis=1, keepdims=True)
        column = jnp.sum(jnp.where(lane_id == j, full, 0.0), axis=1, keepdims=True)
        factor = jnp.where(row_id[:, 0:1] > j, column / pivot, 0.0)
        elim[...] = full - factor * row
        return 0

    lax.fori_loop(0, RANK - 1, eliminate, 0)

    total = ys[own_rows, :]
    for copy in copies:
        copy.wait_recv()
    for d in range(1, NZ):
        total = total + rsy[d]
    yf[own_rows, mine(c)] = total
    for copy in copies:
        copy.wait_send()
    copies, arrivals = gather(lambda j: yf.at[pl.ds(aligned(j, 8), 8), mine(c)], yag_s, yag_r)
    merges(4)
    done = elim[...]
    diagonal = jnp.sum(jnp.where(lane_id == row_id, done, 0.0), axis=1, keepdims=True)
    inverse = done[:, RANK:] / jnp.sqrt(diagonal)
    k = dp % 8
    window = left[dp // 8, :, pl.ds(aligned(k, 128), 256)]
    own_left = pltpu.roll(window, (256 - 16 * k) % 256, 1)[:, 0:CHUNK]
    own_basis = mm32(inverse, own_left, NN)
    second_start()
    for copy in arrivals:
        copy.wait_recv()
    for copy in copies:
        copy.wait_send()

    def given(core):
        return yf.at[:, pl.ds(pl.multiple_of(core * 640, 128), 512)]

    pair = exchange(given(c), given(c), 3)
    pair.start()
    second_merges()
    exchange(given(c), given(1 - c), 3).wait_recv()
    pair.wait_send()
    loads[4].wait()
    for t in range(3):
        columns = pl.ds(t * TILE, TILE)
        right = mm32(inverse, yf[:, columns], NN) * (1.0 / NDP)
        right_ref[:, columns] = right
        mom_ref[:, columns] = DECAY * momentum[:, columns] + mm32(own_basis, right, TN)
    feature_finish()

    for s in range(5):
        for way in (0, 1):
            if s < 4:
                ring_copy(way, s + 1).wait_send()
            if way in ways_of(s):
                pair_copy(way, s, c).wait_send()

    def drain(j, _):
        for h in range(2):
            first.drain(h, j)
        return 0

    lax.fori_loop(0, NDP, drain, 0)

    def drain_second(k, _):
        for h in range(2):
            second.drain(h, own_block(h, k))
        return 0

    lax.fori_loop(0, 4, drain_second, 0)


def fused(tokens, cot, weight, carried, momentum, q_t):
    f32, bf16 = jnp.float32, jnp.bfloat16
    dma = pltpu.SemaphoreType.DMA
    hbm = pl.BlockSpec(memory_space=pl.ANY)
    vmem = pl.BlockSpec(memory_space=pltpu.VMEM)
    return pl.pallas_call(
        fused_kernel,
        out_shape=(
            jax.ShapeDtypeStruct((CHUNK, 768), f32),
            jax.ShapeDtypeStruct((RANK, 1152), f32),
            jax.ShapeDtypeStruct((CHUNK, 1152), f32),
        ),
        in_specs=[hbm] * 5 + [vmem],
        out_specs=(vmem, vmem, vmem),
        scratch_shapes=[
            pltpu.VMEM((768, 2304), bf16),
            pltpu.VMEM((768, 1152), bf16),
            pltpu.VMEM((2304, 1152), bf16),
            pltpu.VMEM((CHUNK, 1152), f32),
            pltpu.VMEM((192, 1152), bf16),
            pltpu.VMEM((192, 768), bf16),
            pltpu.VMEM((2, RANK, 1152), f32),
            pltpu.VMEM((RANK, 1152), f32),
            pltpu.VMEM((RANK, 1152), f32),
            pltpu.VMEM((NZ, 8, 1152), f32),
            pltpu.VMEM((2, RANK, 1152), f32),
            pltpu.VMEM((192, 2304), bf16),
            pltpu.VMEM((RANK, 1152), f32),
            pltpu.VMEM((RANK, 640), f32),
            pltpu.VMEM((RANK, 640), f32),
            pltpu.VMEM((NZ, 8, 640), f32),
            pltpu.VMEM((RANK, 1152), f32),
            pltpu.VMEM((RANK, 128), f32),
            pltpu.VMEM((2304, 1152), bf16),
            pltpu.VMEM((2, 2304, TILE), f32),
            pltpu.VMEM((2, 2, 4, CHUNK, TILE), f32),
            pltpu.VMEM((2, 2, 4, HALF, TILE), f32),
            pltpu.VMEM((2, 2, 1, CHUNK, TILE), f32),
            pltpu.VMEM((2, 2, 1, HALF, TILE), f32),
            dma((5,)),
            dma((8,)),
        ]
        + [dma((NZ,))] * 8
        + [
            dma((2, 5)),
            dma((2, 5)),
            dma((2, 5)),
            dma((2, 5)),
            dma((2, NDP, 2)),
            dma((2, 2, 4, 2)),
            dma((2, 2, 4)),
            dma((2, NDP, 2)),
            dma((2, 2, 1, 2)),
            dma((2, 2, 1)),
        ],
        compiler_params=pltpu.CompilerParams(
            collective_id=0, has_side_effects=True, vmem_limit_bytes=56 * 2**20
        ),
        cost_estimate=pl.CostEstimate(
            flops=8 * 10**9, bytes_accessed=14 * 10**6, transcendentals=0
        ),
        name="fused",
    )(tokens, cot, weight, carried, momentum, q_t)


def body(tokens, up_cotangent, up_weight, carried, momentum, q_start):
    feature_t, right_t, new_momentum = fused(
        tokens, up_cotangent, up_weight, carried[0], momentum, q_start.T
    )
    return (feature_t.T, right_t.T, new_momentum)


def solution(mesh):
    placed = (
        P("dp", None),
        P("dp", "mp"),
        P("dp", "mp"),
        P("dp", None, "mp"),
        P("dp", "mp"),
        P("mp", None),
    )
    return jax.shard_map(
        body,
        mesh=mesh,
        in_specs=placed,
        out_specs=(P("dp", "mp"), P("mp", None), P("dp", "mp")),
        check_vma=False,
    )
```

time: 162 us -> 97.2 us (0.60)
  waiting for transfers between devices: 81.3 us -> 0 us
  Pallas kernels: 49.9 us -> 89.9 us
  between operations: 14 us -> 0.64 us
  matrix products: 10.8 us -> 0 us
    all_gather x1 -> x0, waiting for transfers between devices: 48.2 us -> none  [body(): lax.all_gather(up_weight, 'dp', axis=0, tiled=True)]
    pallas_call x1, Pallas kernels: 49.9 us -> 89.9 us  [fused(): pl.pallas_call(fused_kernel, out_shape=(jax.ShapeDtypeStruct((CHUNK, 768)...]
    reduce_scatter x1 -> x0, waiting for transfers between devices: 32.4 us -> none  [body(): lax.psum_scatter(partial_value, 'mp', scatter_dimension=1, tiled=True)]
    dot_general x1 -> x0, matrix products: 10.8 us -> none  [body(): lax.dot_general(up_cotangent, lax.all_gather(up_weight, 'dp', axis=0, til...]
    unnamed x8 -> x3, local copies, waits for them, and re-layouts: 4.11 us -> 5.47 us
  transfers between devices with their start and end apart: 2 -> 0, of which waited for: 2 -> 0; matrix products, arithmetic and copies ran while one was open for 0% -> 0% of each run, Pallas kernels for 31% -> 0%
where the time goes in v2:
time: 97.2 us; the launch traced here: 96 us
  Pallas kernels  89.9 us (92%)
  local copies, waits for them, and re-layouts  5.47 us (6%)
    pallas_call x1, Pallas kernels, fused(): pl.pallas_call(fused_kernel, out_shape=(jax.ShapeDtypeStruct((CHUNK, 768)...  89.9 us
    unnamed x3, local copies, waits for them, and re-layouts  5.47 us

profile of v2, /device:TPU:12, one launch (start us, length us, event | category | flops | bytes accessed | tf_op | source)
XLA Modules:
  0.0 96.0 jit_solution(3756745229202509810)
XLA Ops:
  0.6 89.9 %fused.1 = (f32[144,768]{1,0:T(8,128)}, f32[64,1152]{1,0:T(8,128)}, f32[144,1152]{1,0:T(8,128)}) custom-call(bf16[768,2304]{1,0:T(8,128)(2,1)} %tokens_hbm.1, bf16[768,1152]{1,0:T(8,128)(2,1)} %cot_hbm.1, bf16[144,1152]{1,0:T(8,128)(2,1)} %weight_hbm.1, bf16[2304,1152]{1,0:T(8,128)(2,1)} %bitcast.6, f32[144,1152]{1,0:T(8,128)} %momentum_hbm.1, ...), custom_call_target="tpu_custom_call" | custom-call | flops 8000000000 | bytes 14000000 | tf_op jit(solution)/shard_map/fused/pallas_call | solution.py:464
  90.5 1.8 %copy.12 = f32[768,144]{0,1:T(8,128)} copy(f32[768,144]{0,1:T(8,128)} %bitcast.4) | data formatting | bytes 884736
  92.3 1.7 %copy.13 = f32[1152,64]{0,1:T(8,128)} copy(f32[1152,64]{0,1:T(8,128)} %bitcast.5) | data formatting | bytes 589824
  94.0 2.0 %copy.14 = f32[144,1152]{1,0:T(8,128)} copy(f32[144,1152]{1,0:T(8,128)} %get-tuple-element.14) | data formatting | bytes 1327104

commit v3 on v2

--- a/solution.py
+++ b/solution.py
@@ -15,6 +15,7 @@
 RANK = 64
 TILE = 384
 FAR_FIRST = (4, 3, 5, 2, 6, 1, 7)
+NEAR_FIRST = (1, 7, 2, 6, 3, 5, 4)
 CHUNK = 144
 HALF = 72
 SPLIT = 80
@@ -53,6 +54,7 @@
     yp, sib_y, ys, rsy, yf, elim,
     weight, part, r1, rl1, r2, rl2,
     load_sem, sib_sem, rs_s, rs_r, ag_s, ag_r, yrs_s, yrs_r, yag_s, yag_r,
+    fw_s, fw_r, yfw_s, yfw_r,
     w_s, w_r, ws_s, ws_r, f1_s, r1_r, rl1_r, f2_s, r2_r, rl2_r,
 ):
     dp = lax.axis_index("dp")
@@ -171,13 +173,14 @@
                 xydev(self.axis(h), 1 if way == 0 else 3),
             )
 
-        def plain(self, h, j):
-            far = self.distance(h, j)
-
-            @pl.when(far == 2)
+        def far(self, h, j):
+            @pl.when(self.distance(h, j) == 2)
             def _():
                 self.send(h, j, True, False, 0).start()
                 self.send(h, j, False, False, 1).start()
+
+        def near(self, h, j):
+            far = self.distance(h, j)
 
             @pl.when(far == 1)
             def _():
@@ -232,38 +235,45 @@
     def place_of(way, s):
         return (z - s + NZ) % NZ if way == 0 else (z + s) % NZ
 
-    def partials(s):
-        for way in ways_of(s):
-            place = place_of(way, s)
-            pair_copy(way, s, 1 - c).wait_recv()
-            rows = pl.ds(pl.multiple_of(place * (2 * CHUNK), 16), 2 * CHUNK)
-            for h in range(2):
-                part[h, rows, :] = mm(weight[rows, :], cot[pl.ds(h * TILE, TILE), :], NT)
-            for h in range(2):
-                for b in range(2):
-                    first.plain(h, place * 2 + b)
-
-    def merges(s):
+    def units_of(s):
         for way in ways_of(s):
             for b in range(2):
                 for h in range(2):
-                    first.merge(h, place_of(way, s) * 2 + b)
+                    yield h, place_of(way, s) * 2 + b
+
+    def partials(s):
+        for way in ways_of(s):
+            pair_copy(way, s, 1 - c).wait_recv()
+            rows = pl.ds(pl.multiple_of(place_of(way, s) * (2 * CHUNK), 16), 2 * CHUNK)
+            for h in range(2):
+                part[h, rows, :] = mm(weight[rows, :], cot[pl.ds(h * TILE, TILE), :], NT)
+        for h, j in units_of(s):
+            first.far(h, j)
+        for h, j in units_of(s):
+            first.near(h, j)
+
+    def merges(s):
+        for h, j in units_of(s):
+            first.merge(h, j)
+
+    def completes(s):
+        for h, j in units_of(s):
+
+            @pl.when(first.distance(h, j) == 0)
+            def _(h=h, j=j):
+                part[h, pl.ds(pl.multiple_of(j * CHUNK, 8), CHUNK), :] = first.collect(h, j)
+                second.far(h, j)
+                second.near(h, j)
+
+    def second_merges(s):
+        for h, j in units_of(s):
+
+            @pl.when(first.distance(h, j) == 0)
+            def _(h=h, j=j):
+                second.merge(h, j)
 
     def own_block(h, k):
         return x * 4 + k if h == 0 else k * 4 + y
-
-    def second_start():
-        for k in range(4):
-            for h in range(2):
-                j = own_block(h, k)
-                total = first.collect(h, j)
-                part[h, pl.ds(pl.multiple_of(j * CHUNK, 8), CHUNK), :] = total
-                second.plain(h, j)
-
-    def second_merges():
-        for k in range(4):
-            for h in range(2):
-                second.merge(h, own_block(h, k))
 
     def feature_finish():
         for h in range(2):
@@ -281,13 +291,14 @@
     loads[2].wait()
     loads[3].wait()
 
-    def left_tile(t, _):
-        columns = pl.ds(aligned(t, TILE), TILE)
-        value = mm(q3[...], carried[columns, :], NT) + mm(t3[...], tokens[:, columns], NN)
-        lp[t // 3, :, pl.ds(aligned(t % 3, TILE), TILE)] = fold3(value)
-        return 0
-
-    lax.fori_loop(0, 6, left_tile, 0)
+    def left_half(h):
+        def tile(t, _):
+            columns = pl.ds(aligned(h * 3 + t, TILE), TILE)
+            value = mm(q3[...], carried[columns, :], NT) + mm(t3[...], tokens[:, columns], NN)
+            lp[h, :, pl.ds(aligned(t, TILE), TILE)] = fold3(value)
+            return 0
+
+        lax.fori_loop(0, 3, tile, 0)
 
     def exchange(src, dst, slot):
         return remote(src, dst, sib_sem.at[2 * slot], sib_sem.at[2 * slot + 1], sib)
@@ -303,26 +314,55 @@
             copies.append(copy)
         return copies
 
-    def gather(block_of, send, recv):
-        copies, arrivals = [], []
+    def gather(block_of, send, recv, given_of, pass_send, pass_recv):
+        copies = []
         for d in FAR_FIRST:
             copy = remote(block_of(z), block_of(z), send.at[d], recv.at[d], zdev(d))
             copy.start()
             copies.append(copy)
-            arrivals.append(
-                remote(block_of(z), block_of((z - d + NZ) % NZ), send.at[d], recv.at[d], zdev(d))
-            )
-        return copies, arrivals
-
+
+        def give(d):
+            rows = given_of((z - d + NZ) % NZ, c)
+            copy = remote(rows, rows, pass_send.at[d], pass_recv.at[d], sib)
+            copy.start()
+            copies.append(copy)
+
+        give(0)
+
+        def finish():
+            for d in NEAR_FIRST:
+                rows = block_of((z - d + NZ) % NZ)
+                remote(rows, rows, send.at[d], recv.at[d], zdev(d)).wait_recv()
+                give(d)
+
+        def taken():
+            for d in (0,) + NEAR_FIRST:
+                rows = given_of((z - d + NZ) % NZ, 1 - c)
+                remote(rows, rows, pass_send.at[d], pass_recv.at[d], sib).wait_recv()
+
+        def sent():
+            for copy in copies:
+                copy.wait_send()
+
+        return finish, taken, sent
+
+    left_half(1 - c)
     pair = exchange(lp.at[1 - c], sib_l, 0)
     pair.start()
+    left_half(c)
     partials(0)
+    ring_step(1)
+    partials(1)
     pair.wait()
     cs[...] = lp[c] + sib_l[...]
+    ring_step(2)
     copies = scatter(cs, rsl, rs_s, rs_r)
-    ring_step(1)
-    partials(1)
     merges(0)
+    partials(2)
+    merges(1)
+    completes(0)
+    ring_step(3)
+    partials(3)
     own_rows = pl.ds(aligned(z, 8), 8)
     total = cs[own_rows, :]
     for copy in copies:
@@ -330,49 +370,59 @@
     for d in range(1, NZ):
         total = total + rsl[d]
     left[c, own_rows, :] = total * (1.0 / NDP)
-    for copy in copies:
-        copy.wait_send()
-    copies, arrivals = gather(lambda j: left.at[c, pl.ds(aligned(j, 8), 8), :], ag_s, ag_r)
-    ring_step(2)
-    partials(2)
-    merges(1)
-    for copy in arrivals:
-        copy.wait_recv()
-    for copy in copies:
-        copy.wait_send()
-    pair = exchange(left.at[c], left.at[c], 1)
-    pair.start()
-    ring_step(3)
-    exchange(left.at[c], left.at[1 - c], 1).wait_recv()
-    pair.wait_send()
-
-    for h in range(2):
-        left3[:, h * 1152 : (h + 1) * 1152] = split3(left[h])
+
+    def left_block(j, core):
+        return left.at[core, pl.ds(aligned(j, 8), 8), :]
+
+    finish, taken, sent = gather(
+        lambda j: left_block(j, c), ag_s, ag_r, left_block, fw_s, fw_r
+    )
+    ring_step(4)
+    partials(4)
+    merges(2)
+    completes(1)
+    finish()
+
+    def half_columns(h):
+        return pl.ds(aligned(h, 1152), 1152)
+
+    left3[:, half_columns(c)] = split3(left[c])
+    t2 = []
+    for t in range(2):
+        t2.append(
+            mm(left3[:, half_columns(c)], tokens[pl.ds(t * TILE, TILE), half_columns(c)], NT)
+        )
+    taken()
+    left3[:, half_columns(1 - c)] = split3(left[1 - c])
     for t in range(2):
         rows = pl.ds(t * TILE, TILE)
-        t3[:, rows] = split3(fold3(mm(left3[...], tokens[rows, :], NT)))
-
-    def y_tile(t, _):
+        rest = mm(left3[:, half_columns(1 - c)], tokens[rows, half_columns(1 - c)], NT)
+        t3[:, rows] = split3(fold3(t2[t] + rest))
+
+    def y_tile(t):
         columns = pl.ds(aligned(t, TILE), TILE)
         value = mm(left3[...], carried[:, columns], NN) + mm(t3[...], cot[:, columns], NN)
         yp[:, columns] = fold3(value)
+
+    def y_first(i, _):
+        y_tile(c * i + (1 - c) * (2 - i))
         return 0
-
-    lax.fori_loop(0, 3, y_tile, 0)
 
     def mine(core):
         return pl.ds(pl.multiple_of(core * 512, 128), 640)
 
-    pair = exchange(yp.at[:, mine(1 - c)], sib_y, 2)
+    lax.fori_loop(0, 2, y_first, 0)
+    pair = exchange(yp.at[:, mine(1 - c)], sib_y, 1)
     pair.start()
-    partials(3)
-    merges(2)
+    y_tile(2 * c)
     pair.wait()
     ys[...] = yp[:, mine(c)] + sib_y[...]
-    copies = scatter(ys, rsy, yrs_s, yrs_r)
-    ring_step(4)
-    partials(4)
+    copies += scatter(ys, rsy, yrs_s, yrs_r)
     merges(3)
+    completes(2)
+    second_merges(0)
+    merges(4)
+    second_merges(1)
 
     products = mm(left3[...], left3[...], NT)
     gram = jnp.zeros((RANK, RANK), jnp.float32)
@@ -396,15 +446,18 @@
     lax.fori_loop(0, RANK - 1, eliminate, 0)
 
     total = ys[own_rows, :]
-    for copy in copies:
+    for copy in copies[7:]:
         copy.wait_recv()
     for d in range(1, NZ):
         total = total + rsy[d]
     yf[own_rows, mine(c)] = total
-    for copy in copies:
-        copy.wait_send()
-    copies, arrivals = gather(lambda j: yf.at[pl.ds(aligned(j, 8), 8), mine(c)], yag_s, yag_r)
-    merges(4)
+
+    def y_given(j, core):
+        return yf.at[pl.ds(aligned(j, 8), 8), pl.ds(pl.multiple_of(core * 640, 128), 512)]
+
+    y_finish, y_taken, y_sent = gather(
+        lambda j: yf.at[pl.ds(aligned(j, 8), 8), mine(c)], yag_s, yag_r, y_given, yfw_s, yfw_r
+    )
     done = elim[...]
     diagonal = jnp.sum(jnp.where(lane_id == row_id, done, 0.0), axis=1, keepdims=True)
     inverse = done[:, RANK:] / jnp.sqrt(diagonal)
@@ -412,28 +465,25 @@
     window = left[dp // 8, :, pl.ds(aligned(k, 128), 256)]
     own_left = pltpu.roll(window, (256 - 16 * k) % 256, 1)[:, 0:CHUNK]
     own_basis = mm32(inverse, own_left, NN)
-    second_start()
-    for copy in arrivals:
-        copy.wait_recv()
-    for copy in copies:
-        copy.wait_send()
-
-    def given(core):
-        return yf.at[:, pl.ds(pl.multiple_of(core * 640, 128), 512)]
-
-    pair = exchange(given(c), given(c), 3)
-    pair.start()
-    second_merges()
-    exchange(given(c), given(1 - c), 3).wait_recv()
-    pair.wait_send()
+    completes(3)
+    second_merges(2)
+    y_finish()
+    completes(4)
+    second_merges(3)
+    y_taken()
     loads[4].wait()
     for t in range(3):
         columns = pl.ds(t * TILE, TILE)
         right = mm32(inverse, yf[:, columns], NN) * (1.0 / NDP)
         right_ref[:, columns] = right
         mom_ref[:, columns] = DECAY * momentum[:, columns] + mm32(own_basis, right, TN)
+    second_merges(4)
     feature_finish()
 
+    for copy in copies:
+        copy.wait_send()
+    sent()
+    y_sent()
     for s in range(5):
         for way in (0, 1):
             if s < 4:
@@ -496,9 +546,9 @@
             pltpu.VMEM((2, 2, 1, CHUNK, TILE), f32),
             pltpu.VMEM((2, 2, 1, HALF, TILE), f32),
             dma((5,)),
-            dma((8,)),
+            dma((4,)),
         ]
-        + [dma((NZ,))] * 8
+        + [dma((NZ,))] * 12
         + [
             dma((2, 5)),
             dma((2, 5)),
@@ -521,10 +571,37 @@
     )(tokens, cot, weight, carried, momentum, q_t)
 
 
+def hand_on_kernel(*refs):
+    sources, results, held, sems = refs[0:3], refs[3:6], refs[6:9], refs[9]
+    loads = [pltpu.make_async_copy(sources[i], held[i], sems.at[i]) for i in range(3)]
+    stores = [pltpu.make_async_copy(held[i], results[i], sems.at[3 + i]) for i in range(3)]
+    for copy in loads:
+        copy.start()
+    for load, store in zip(loads, stores):
+        load.wait()
+        store.start()
+    for copy in stores:
+        copy.wait()
+
+
+def hand_on(*arrays):
+    hbm = pl.BlockSpec(memory_space=pl.ANY)
+    return pl.pallas_call(
+        hand_on_kernel,
+        out_shape=tuple(jax.ShapeDtypeStruct(a.shape, a.dtype) for a in arrays),
+        in_specs=[hbm] * 3,
+        out_specs=(hbm,) * 3,
+        scratch_shapes=[pltpu.VMEM(a.shape, a.dtype) for a in arrays]
+        + [pltpu.SemaphoreType.DMA((6,))],
+        name="hand_on",
+    )(*arrays)
+
+
 def body(tokens, up_cotangent, up_weight, carried, momentum, q_start):
     feature_t, right_t, new_momentum = fused(
         tokens, up_cotangent, up_weight, carried[0], momentum, q_start.T
     )
+    feature_t, right_t, new_momentum = hand_on(feature_t, right_t, new_momentum)
     return (feature_t.T, right_t.T, new_momentum)
 
 

time: 97.2 us -> 92.7 us (0.954); the launches traced: 96 us -> 92.6 us
  local copies, waits for them, and re-layouts: 5.47 us -> 0 us
  Pallas kernels: 89.9 us -> 91.8 us
    unnamed x3 -> x0, local copies, waits for them, and re-layouts: 5.47 us -> none
    pallas_call x0 -> x1, Pallas kernels: none -> 2.21 us  [hand_on(): pl.pallas_call(hand_on_kernel, out_shape=tuple((jax.ShapeDtypeStruct(a.sh...]
where the time goes in v3:
time: 92.7 us; the launch traced here: 92.6 us
  Pallas kernels  91.8 us (99%)
    pallas_call x1, Pallas kernels, fused(): pl.pallas_call(fused_kernel, out_shape=(jax.ShapeDtypeStruct((CHUNK, 768)...  89.6 us
    pallas_call x1, Pallas kernels, hand_on(): pl.pallas_call(hand_on_kernel, out_shape=tuple((jax.ShapeDtypeStruct(a.sh...  2.21 us

profile of v3, /device:TPU:12, one launch (start us, length us, event | category | flops | bytes accessed | tf_op | source)
XLA Modules:
  0.0 92.6 jit_solution(14052434043899292416)
XLA Ops:
  0.6 89.6 %fused.1 = (f32[144,768]{1,0:T(8,128)}, f32[64,1152]{1,0:T(8,128)}, f32[144,1152]{1,0:T(8,128)}) custom-call(bf16[768,2304]{1,0:T(8,128)(2,1)} %tokens_hbm.1, bf16[768,1152]{1,0:T(8,128)(2,1)} %cot_hbm.1, bf16[144,1152]{1,0:T(8,128)(2,1)} %weight_hbm.1, bf16[2304,1152]{1,0:T(8,128)(2,1)} %bitcast.4, f32[144,1152]{1,0:T(8,128)} %momentum_hbm.1, ...), custom_call_target="tpu_custom_call" | custom-call | flops 8000000000 | bytes 14000000 | tf_op jit(solution)/shard_map/fused/pallas_call | solution.py:514
  90.2 2.2 %hand_on.1 = (f32[144,768]{1,0:T(8,128)}, f32[64,1152]{1,0:T(8,128)}, f32[144,1152]{1,0:T(8,128)}) custom-call(f32[144,768]{1,0:T(8,128)} %get-tuple-element.9.refs_0_, f32[64,1152]{1,0:T(8,128)} %get-tuple-element.10.refs_1_, f32[144,1152]{1,0:T(8,128)} %get-tuple-element.11.refs_2_), custom_call_target="tpu_custom_call" | custom-call | tf_op jit(solution)/shard_map/hand_on/pallas_call | solution.py:589

commit v4 on v3

--- a/solution.py
+++ b/solution.py
@@ -279,14 +279,15 @@
         for h in range(2):
             feature_ref[:, pl.ds(h * TILE, TILE)] = second.collect(h, mp)
 
+    loads[0].wait()
+    pl.semaphore_wait(barrier, NZ + 4)
+    ring_step(0)
+    loads[1].wait()
+    partials(0)
     q3[...] = split3(q_ref[...])
-    loads[1].wait()
     for t in range(2):
         rows = pl.ds(t * TILE, TILE)
         t3[:, rows] = split3(fold3(mm(q3[...], cot[rows, :], NT)))
-    loads[0].wait()
-    pl.semaphore_wait(barrier, NZ + 4)
-    ring_step(0)
 
     loads[2].wait()
     loads[3].wait()
@@ -349,20 +350,20 @@
     left_half(1 - c)
     pair = exchange(lp.at[1 - c], sib_l, 0)
     pair.start()
-    left_half(c)
-    partials(0)
     ring_step(1)
     partials(1)
+    left_half(c)
     pair.wait()
     cs[...] = lp[c] + sib_l[...]
     ring_step(2)
+    partials(2)
+    ring_step(3)
     copies = scatter(cs, rsl, rs_s, rs_r)
     merges(0)
-    partials(2)
+    partials(3)
     merges(1)
-    completes(0)
-    ring_step(3)
-    partials(3)
+    ring_step(4)
+    partials(4)
     own_rows = pl.ds(aligned(z, 8), 8)
     total = cs[own_rows, :]
     for copy in copies:
@@ -377,10 +378,8 @@
     finish, taken, sent = gather(
         lambda j: left_block(j, c), ag_s, ag_r, left_block, fw_s, fw_r
     )
-    ring_step(4)
-    partials(4)
     merges(2)
-    completes(1)
+    completes(0)
     finish()
 
     def half_columns(h):
@@ -419,10 +418,10 @@
     ys[...] = yp[:, mine(c)] + sib_y[...]
     copies += scatter(ys, rsy, yrs_s, yrs_r)
     merges(3)
-    completes(2)
+    completes(1)
     second_merges(0)
     merges(4)
-    second_merges(1)
+    completes(2)
 
     products = mm(left3[...], left3[...], NT)
     gram = jnp.zeros((RANK, RANK), jnp.float32)
@@ -465,6 +464,7 @@
     window = left[dp // 8, :, pl.ds(aligned(k, 128), 256)]
     own_left = pltpu.roll(window, (256 - 16 * k) % 256, 1)[:, 0:CHUNK]
     own_basis = mm32(inverse, own_left, NN)
+    second_merges(1)
     completes(3)
     second_merges(2)
     y_finish()

time: 92.7 us -> 88.8 us (0.958)
  Pallas kernels: 91.8 us -> 87.9 us
    pallas_call x1, Pallas kernels: 89.6 us -> 85.7 us  [fused(): pl.pallas_call(fused_kernel, out_shape=(jax.ShapeDtypeStruct((CHUNK, 768)...]
where the time goes in v4:
time: 88.8 us; the launch traced here: 88.7 us
  Pallas kernels  87.9 us (99%)
    pallas_call x1, Pallas kernels, fused(): pl.pallas_call(fused_kernel, out_shape=(jax.ShapeDtypeStruct((CHUNK, 768)...  85.7 us
    pallas_call x1, Pallas kernels, hand_on(): pl.pallas_call(hand_on_kernel, out_shape=tuple((jax.ShapeDtypeStruct(a.sh...  2.21 us

profile of v4, /device:TPU:12, one launch (start us, length us, event | category | flops | bytes accessed | tf_op | source)
XLA Modules:
  0.0 88.7 jit_solution(16305289704526640277)
XLA Ops:
  0.6 85.7 %fused.1 = (f32[144,768]{1,0:T(8,128)}, f32[64,1152]{1,0:T(8,128)}, f32[144,1152]{1,0:T(8,128)}) custom-call(bf16[768,2304]{1,0:T(8,128)(2,1)} %tokens_hbm.1, bf16[768,1152]{1,0:T(8,128)(2,1)} %cot_hbm.1, bf16[144,1152]{1,0:T(8,128)(2,1)} %weight_hbm.1, bf16[2304,1152]{1,0:T(8,128)(2,1)} %bitcast.4, f32[144,1152]{1,0:T(8,128)} %momentum_hbm.1, ...), custom_call_target="tpu_custom_call" | custom-call | flops 8000000000 | bytes 14000000 | tf_op jit(solution)/shard_map/fused/pallas_call | solution.py:514
  86.3 2.2 %hand_on.1 = (f32[144,768]{1,0:T(8,128)}, f32[64,1152]{1,0:T(8,128)}, f32[144,1152]{1,0:T(8,128)}) custom-call(f32[144,768]{1,0:T(8,128)} %get-tuple-element.9.refs_0_, f32[64,1152]{1,0:T(8,128)} %get-tuple-element.10.refs_1_, f32[144,1152]{1,0:T(8,128)} %get-tuple-element.11.refs_2_), custom_call_target="tpu_custom_call" | custom-call | tf_op jit(solution)/shard_map/hand_on/pallas_call | solution.py:589

commit v5 on v4

--- a/solution.py
+++ b/solution.py
@@ -381,6 +381,8 @@
     merges(2)
     completes(0)
     finish()
+    merges(3)
+    merges(4)
 
     def half_columns(h):
         return pl.ds(aligned(h, 1152), 1152)
@@ -417,10 +419,8 @@
     pair.wait()
     ys[...] = yp[:, mine(c)] + sib_y[...]
     copies += scatter(ys, rsy, yrs_s, yrs_r)
-    merges(3)
     completes(1)
     second_merges(0)
-    merges(4)
     completes(2)
 
     products = mm(left3[...], left3[...], NT)

time: 88.8 us -> 90.7 us (1.021)
  Pallas kernels: 87.9 us -> 89.8 us
    pallas_call x1, Pallas kernels: 85.7 us -> 87.6 us  [fused(): pl.pallas_call(fused_kernel, out_shape=(jax.ShapeDtypeStruct((CHUNK, 768)...]
where the time goes in v5:
time: 90.7 us; the launch traced here: 90.6 us
  Pallas kernels  89.8 us (99%)
    pallas_call x1, Pallas kernels, fused(): pl.pallas_call(fused_kernel, out_shape=(jax.ShapeDtypeStruct((CHUNK, 768)...  87.6 us
    pallas_call x1, Pallas kernels, hand_on(): pl.pallas_call(hand_on_kernel, out_shape=tuple((jax.ShapeDtypeStruct(a.sh...  2.21 us

profile of v5, /device:TPU:12, one launch (start us, length us, event | category | flops | bytes accessed | tf_op | source)
XLA Modules:
  0.0 90.6 jit_solution(12098472267493285343)
XLA Ops:
  0.6 87.6 %fused.1 = (f32[144,768]{1,0:T(8,128)}, f32[64,1152]{1,0:T(8,128)}, f32[144,1152]{1,0:T(8,128)}) custom-call(bf16[768,2304]{1,0:T(8,128)(2,1)} %tokens_hbm.1, bf16[768,1152]{1,0:T(8,128)(2,1)} %cot_hbm.1, bf16[144,1152]{1,0:T(8,128)(2,1)} %weight_hbm.1, bf16[2304,1152]{1,0:T(8,128)(2,1)} %bitcast.4, f32[144,1152]{1,0:T(8,128)} %momentum_hbm.1, ...), custom_call_target="tpu_custom_call" | custom-call | flops 8000000000 | bytes 14000000 | tf_op jit(solution)/shard_map/fused/pallas_call | solution.py:514
  88.2 2.2 %hand_on.1 = (f32[144,768]{1,0:T(8,128)}, f32[64,1152]{1,0:T(8,128)}, f32[144,1152]{1,0:T(8,128)}) custom-call(f32[144,768]{1,0:T(8,128)} %get-tuple-element.9.refs_0_, f32[64,1152]{1,0:T(8,128)} %get-tuple-element.10.refs_1_, f32[144,1152]{1,0:T(8,128)} %get-tuple-element.11.refs_2_), custom_call_target="tpu_custom_call" | custom-call | tf_op jit(solution)/shard_map/hand_on/pallas_call | solution.py:589
